TPU v7x, 128 devices: a whole 4x4x4 slice. The times are simulated.
128 devices in a mesh: replica: 4 (over z_hi, core), expert: 8 (over y, z_lo), tensor: 4 (over x).
Axes of the slice: x: 4, y: 4, z: 4 (z_hi: 2, z_lo: 2; z = z_hi * 2 + z_lo), core: 2. Of those that a mesh axis runs over, the one named last changes fastest.
Arguments:
- states: bfloat16 [512, 4096], P(('replica', 'expert'), 'tensor'), may hold values from -6 to 6
- gain: float32 [4096], replicated, may hold values from 0.1 to 1.9
- route_ids: int32 [3, 512, 4], P(None, ('replica', 'expert')), may hold values from 0 to 15, all different within a row; in each aligned block of 16 rows (0 to 15, 16 to 31, ..., all dimensions but the last counted through in order) at most 8 rows name the same one
- route_weights: float32 [3, 512, 4], P(None, ('replica', 'expert')), may hold values from 0.1 to 1
- gate_w: bfloat16 [16, 4096, 1536], P('expert', None, 'tensor'), may hold values from -0.09375 to 0.09375
- up_w: bfloat16 [16, 4096, 1536], P('expert', None, 'tensor'), may hold values from -0.09375 to 0.09375
- down_w: bfloat16 [16, 1536, 4096], P('expert', 'tensor'), may hold values from -0.15625 to 0.15625
- gate_a: bfloat16 [16, 32, 4096], P('expert', 'replica'), may hold values from -0.09375 to 0.09375
- gate_b: bfloat16 [16, 32, 1536], P('expert', 'replica', 'tensor'), may hold values from -0.5 to 0.5
- up_a: bfloat16 [16, 32, 4096], P('expert', 'replica'), may hold values from -0.09375 to 0.09375
- up_b: bfloat16 [16, 32, 1536], P('expert', 'replica', 'tensor'), may hold values from -0.5 to 0.5
- down_a: bfloat16 [16, 32, 1536], P('expert', 'replica', 'tensor'), may hold values from -0.15625 to 0.15625
- down_b: bfloat16 [16, 32, 4096], P('expert', 'replica'), may hold values from -0.8984375 to 0.8984375
Outputs:
- new_states: float32 [512, 4096], P(('replica', 'expert'), 'tensor')
- last_update: float32 [512, 4096], P(('replica', 'expert'), 'tensor')
Inputs may be any that keep to these rules, and one draw needn't show every extreme that they name: `route_ids`: each row names 4 different experts. In each step, the 16 rows of one device (aligned blocks of rows) name no expert more than 8 times, and in some blocks one expert exactly 8 times.
All inputs are finite; a program needn't handle non-finite values.
Results may differ from a plain program's by a relative error of at most 0.02.
Values may be sent and summed in bfloat16 or wider, within the bound.
A program may use at most 128 MiB of HBM per device.

v0:
```python
import jax
import jax.numpy as jnp
from jax import lax
from jax.sharding import PartitionSpec as P

EPS = 1e-06


def normalize(rows, gain):
    mean_square = jnp.mean(rows * rows, axis=-1, keepdims=True)
    return (rows * lax.rsqrt(mean_square + EPS) * gain).astype(jnp.bfloat16)


def merge_weight(base, left, right, form):
    delta = jnp.einsum(form, left, right, preferred_element_type=jnp.float32)
    return (base.astype(jnp.float32) + 2.0 * delta).astype(jnp.bfloat16)


def per_device(
    states,
    gain,
    route_ids,
    route_weights,
    gate_w,
    up_w,
    down_w,
    gate_a,
    gate_b,
    up_a,
    up_b,
    down_a,
    down_b,
):
    gate_left, gate_right, up_left, up_right, down_left, down_right = (
        lax.all_gather(gate_a, "replica", axis=1, tiled=True),
        lax.all_gather(gate_b, "replica", axis=1, tiled=True),
        lax.all_gather(up_a, "replica", axis=1, tiled=True),
        lax.all_gather(up_b, "replica", axis=1, tiled=True),
        lax.all_gather(down_a, "replica", axis=1, tiled=True),
        lax.all_gather(down_b, "replica", axis=1, tiled=True),
    )
    merged_gate = merge_weight(gate_w, gate_left, gate_right, "erd,erf->edf")
    merged_up = merge_weight(up_w, up_left, up_right, "erd,erf->edf")
    merged_down = merge_weight(down_w, down_left, down_right, "erf,erd->efd")
    local_experts = gate_w.shape[0]
    expert_devices = lax.axis_size("expert")
    total_experts = local_experts * expert_devices
    row_count = states.shape[0]
    top_count = route_ids.shape[2]
    capacity = 2 * row_count * top_count // total_experts
    slot_count = total_experts * capacity
    positions = jnp.arange(slot_count, dtype=jnp.int32)
    experts_iota = jnp.arange(total_experts, dtype=jnp.int32)
    current = states.astype(jnp.float32)
    update = jnp.zeros((row_count, states.shape[1]), jnp.float32)
    for step in range(route_ids.shape[0]):
        chosen = route_ids[step].reshape(-1)
        onehot = (chosen[:, None] == experts_iota[None, :]).astype(jnp.int32)
        prior = jnp.cumsum(onehot, axis=0) - onehot
        slots = jnp.sum(prior * onehot, axis=1)
        target = (chosen * capacity + slots).reshape(row_count, top_count)
        hits = jnp.any(positions[:, None, None] == target[None, :, :], axis=2)
        raw = route_weights[step]
        mixing = raw / jnp.sum(raw, axis=-1, keepdims=True)
        combine = jnp.sum(
            jnp.where(target[:, :, None] == positions[None, None, :], mixing[:, :, None], 0.0),
            axis=1,
        )
        whole = lax.all_gather(current, "tensor", axis=1, tiled=True)
        normed = normalize(whole, gain)
        outgoing = jnp.dot(
            hits.astype(jnp.bfloat16), normed, preferred_element_type=jnp.float32
        ).astype(jnp.bfloat16)
        outgoing = outgoing.reshape(expert_devices, local_experts, capacity, -1)
        arrived = lax.all_to_all(outgoing, "expert", split_axis=0, concat_axis=0, tiled=True)
        gate = jnp.einsum(
            "njcd,jdf->njcf", arrived, merged_gate, preferred_element_type=jnp.float32
        )
        upper = jnp.einsum("njcd,jdf->njcf", arrived, merged_up, preferred_element_type=jnp.float32)
        hidden = (jax.nn.silu(gate) * upper).astype(jnp.bfloat16)
        partial_value = jnp.einsum(
            "njcf,jfd->njcd", hidden, merged_down, preferred_element_type=jnp.float32
        )
        returned = lax.all_to_all(partial_value, "expert", split_axis=0, concat_axis=0, tiled=True)
        shares = lax.psum_scatter(returned, "tensor", scatter_dimension=3, tiled=True).astype(
            jnp.bfloat16
        )
        update = jnp.dot(
            combine,
            shares.reshape(slot_count, -1).astype(jnp.float32),
            precision=lax.Precision.HIGHEST,
        )
        current = current + update
    return (current, update)


def solution(mesh):
    return jax.shard_map(
        per_device,
        mesh=mesh,
        in_specs=(
            P(("replica", "expert"), "tensor"),
            P(),
            P(None, ("replica", "expert"), None),
            P(None, ("replica", "expert"), None),
            P("expert", None, "tensor"),
            P("expert", None, "tensor"),
            P("expert", "tensor", None),
            P("expert", "replica", None),
            P("expert", "replica", "tensor"),
            P("expert", "replica", None),
            P("expert", "replica", "tensor"),
            P("expert", "replica", "tensor"),
            P("expert", "replica", None),
        ),
        out_specs=(P(("replica", "expert"), "tensor"), P(("replica", "expert"), "tensor")),
        check_vma=False,
    )
```

profile of v0, /device:TPU:0, one launch (start us, length us, event | category | flops | bytes accessed | tf_op | source)
XLA Modules:
  0.0 363.7 jit_solution(11147305317599535612)
XLA Ops:
  7.2 0.7 fusion.84
  8.2 0.2 select_reduce_fusion.5
  8.7 0.8 convert_element_type.72
  9.5 12.7 %all_gather.31 = f32[16,4096]{1,0:T(8,128)S(1)} all-gather(f32[16,1024]{1,0:T(8,128)S(1)} %convert_element_type.72), channel_id=1, replica_groups=mesh['replica'=4,'expert'=8,'tensor'=4] {'tensor'}, dimensions={1}, use_global_device_ids=true | all-gather | bytes 327680 | tf_op jit(solution)/shard_map/all_gather | solution.py:69
  22.1 0.1 multiply_reduce_fusion.2
  22.3 2.2 convolution_convert_fusion.2
  24.5 5.8 %all-to-all-start = ((bf16[8,2,8,4096]{3,2,1,0:T(8,128)(2,1)}), bf16[8,2,8,4096]{3,2,1,0:T(8,128)(2,1)S(1)}, u32[]{:S(2)}, u32[]{:S(2)}) async-start(bf16[8,2,8,4096]{3,2,1,0:T(8,128)(2,1)} %bitcast.7), calls=%async_computation | async-start | bytes 2097152 | tf_op jit(solution)/shard_map/all_to_all | solution.py:75
  30.4 16.6 %all_gather.32 = bf16[2,32,4096]{2,1,0:T(8,128)(2,1)S(1)} all-gather(bf16[2,8,4096]{2,1,0:T(8,128)(2,1)} %param.22), channel_id=1, replica_groups=mesh['replica'=4,'expert'=8,'tensor'=4] {'replica'}, dimensions={1}, use_global_device_ids=true | all-gather | bytes 655360 | tf_op jit(solution)/shard_map/all_gather | solution.py:37
  47.0 6.9 %all_gather.33 = bf16[2,32,384]{2,1,0:T(8,128)(2,1)S(1)} all-gather(bf16[2,8,384]{2,1,0:T(8,128)(2,1)} %param.23), channel_id=1, replica_groups=mesh['replica'=4,'expert'=8,'tensor'=4] {'replica'}, dimensions={1}, use_global_device_ids=true | all-gather | bytes 61440 | tf_op jit(solution)/shard_map/all_gather | solution.py:38
  53.9 6.9 %all_gather.27 = bf16[2,32,384]{2,1,0:T(8,128)(2,1)S(1)} all-gather(bf16[2,8,384]{2,1,0:T(8,128)(2,1)} %param.24), channel_id=1, replica_groups=mesh['replica'=4,'expert'=8,'tensor'=4] {'replica'}, dimensions={1}, use_global_device_ids=true | all-gather | bytes 61440 | tf_op jit(solution)/shard_map/all_gather | solution.py:39
  60.9 9.1 %all_gather.28 = bf16[2,32,4096]{2,1,0:T(8,128)(2,1)S(1)} all-gather(bf16[2,8,4096]{2,1,0:T(8,128)(2,1)} %param.25), channel_id=1, replica_groups=mesh['replica'=4,'expert'=8,'tensor'=4] {'replica'}, dimensions={1}, use_global_device_ids=true | all-gather | bytes 655360 | tf_op jit(solution)/shard_map/all_gather | solution.py:40
  70.0 7.4 %add_convert_fusion = bf16[2,4096,384]{2,1,0:T(8,128)(2,1)} fusion(bf16[2,4096,384]{2,1,0:T(8,128)(2,1)} %param.18, bf16[2,32,4096]{2,1,0:T(8,128)(2,1)S(1)} %all_gather.32, bf16[2,32,384]{2,1,0:T(8,128)(2,1)S(1)} %all_gather.33), kind=kOutput, calls=%fused_computation | convolution fusion | flops 213909504 | bytes 13156352 | tf_op jit(solution)/shard_map/erd,erf->edf/dot_general | solution.py:15
  77.5 4.5 %add_convert_fusion.2 = bf16[2,384,4096]{2,1,0:T(8,128)(2,1)} fusion(bf16[2,384,4096]{2,1,0:T(8,128)(2,1)S(1)} %bitcast.127, bf16[2,32,384]{2,1,0:T(8,128)(2,1)S(1)} %all_gather.27, bf16[2,32,4096]{2,1,0:T(8,128)(2,1)S(1)} %all_gather.28), kind=kOutput, calls=%fused_computation.2 | convolution fusion | flops 213909504 | bytes 13156352 | tf_op jit(solution)/shard_map/erf,erd->efd/dot_general | solution.py:15
  81.9 6.7 %all_gather.30 = bf16[2,32,384]{2,1,0:T(8,128)(2,1)S(1)} all-gather(bf16[2,8,384]{2,1,0:T(8,128)(2,1)S(1)} %copy-done.4), channel_id=1, replica_groups=mesh['replica'=4,'expert'=8,'tensor'=4] {'replica'}, dimensions={1}, use_global_device_ids=true | all-gather | bytes 61440 | tf_op jit(solution)/shard_map/all_gather | solution.py:36
  88.7 8.8 %all_gather.29 = bf16[2,32,4096]{2,1,0:T(8,128)(2,1)S(1)} all-gather(bf16[2,8,4096]{2,1,0:T(8,128)(2,1)S(1)} %copy-done.1), channel_id=1, replica_groups=mesh['replica'=4,'expert'=8,'tensor'=4] {'replica'}, dimensions={1}, use_global_device_ids=true | all-gather | bytes 655360 | tf_op jit(solution)/shard_map/all_gather | solution.py:35
  97.5 4.5 %add_convert_fusion.1 = bf16[2,4096,384]{2,1,0:T(8,128)(2,1)} fusion(bf16[2,4096,384]{2,1,0:T(8,128)(2,1)S(1)} %bitcast.129, bf16[2,32,4096]{2,1,0:T(8,128)(2,1)S(1)} %all_gather.29, bf16[2,32,384]{2,1,0:T(8,128)(2,1)S(1)} %all_gather.30), kind=kOutput, calls=%fused_computation.1 | convolution fusion | flops 213909504 | bytes 13156352 | tf_op jit(solution)/shard_map/erd,erf->edf/dot_general | solution.py:15
  102.0 4.0 %fusion.27 = f32[8,2,8,384]{3,2,0,1:T(8,128)S(1)} fusion(bf16[2,4096,384]{2,1,0:T(8,128)(2,1)} %add_convert_fusion.1, bf16[8,2,8,4096]{3,2,1,0:T(8,128)(2,1)S(1)} %all-to-all-done), kind=kOutput, calls=%fused_computation.27 | convolution fusion | flops 402653184 | bytes 7536640 | tf_op jit(solution)/shard_map/njcd,jdf->njcf/dot_general | solution.py:76
  105.9 4.0 %fusion.54 = bf16[8,2,8,384]{3,2,0,1:T(8,128)(2,1)S(1)} fusion(bf16[2,4096,384]{2,1,0:T(8,128)(2,1)} %add_convert_fusion, bf16[8,2,8,4096]{3,2,1,0:T(8,128)(2,1)S(1)} %all-to-all-done, f32[8,2,8,384]{3,2,0,1:T(8,128)S(1)} %fusion.27), kind=kOutput, calls=%fused_computation.36 | convolution fusion | flops 402948096 | bytes 7634944 | tf_op jit(solution)/shard_map/njcd,jdf->njcf/dot_general | solution.py:79
  109.9 1.2 fusion.18
  111.3 31.8 %all_to_all.30 = f32[8,2,8,4096]{3,2,1,0:T(8,128)} all-to-all(f32[8,2,8,4096]{3,2,1,0:T(8,128)S(1)} %copy.102), channel_id=1, replica_groups=mesh['replica'=4,'expert'=8,'tensor'=4] {'expert'}, dimensions={0} | all-to-all | bytes 4194304 | tf_op jit(solution)/shard_map/all_to_all | solution.py:84
  143.1 0.2 reduce-scatter.6.cloned.1.call-start
  143.9 0.2 select_reduce_fusion.3
  144.5 25.1 %reduce-scatter.4.cloned.1.call-done = f32[8,2,8,1024]{3,2,1,0:T(8,128)} async-done(((f32[8,2,8,4096]{3,2,1,0:T(8,128)}), f32[8,2,8,1024]{3,2,1,0:T(8,128)}) %reduce-scatter.4.cloned.1.call-update) | async-done | bytes 524304 | tf_op jit(solution)/shard_map/reduce_scatter | solution.py:85
  169.7 1.1 convert_element_type.83
  170.7 0.2 convolution_add_fusion.1
  171.0 12.3 %all_gather.34 = f32[16,4096]{1,0:T(8,128)S(1)} all-gather(f32[16,1024]{1,0:T(8,128)S(1)} %convolution_add_fusion.1), channel_id=1, replica_groups=mesh['replica'=4,'expert'=8,'tensor'=4] {'tensor'}, dimensions={1}, use_global_device_ids=true | all-gather | bytes 327680 | tf_op jit(solution)/shard_map/all_gather | solution.py:69
  183.4 0.5 convolution_convert_fusion.1
  183.9 17.8 %all_to_all.31 = bf16[8,2,8,4096]{3,2,1,0:T(8,128)(2,1)S(1)} all-to-all(bf16[8,2,8,4096]{3,2,1,0:T(8,128)(2,1)S(1)} %bitcast.140), channel_id=1, replica_groups=mesh['replica'=4,'expert'=8,'tensor'=4] {'expert'}, dimensions={0} | all-to-all | bytes 2097152 | tf_op jit(solution)/shard_map/all_to_all | solution.py:75
  201.7 4.0 %fusion.30 = f32[8,2,8,384]{3,2,0,1:T(8,128)S(1)} fusion(bf16[2,4096,384]{2,1,0:T(8,128)(2,1)} %add_convert_fusion.1, bf16[8,2,8,4096]{3,2,1,0:T(8,128)(2,1)S(1)} %all_to_all.31), kind=kOutput, calls=%fused_computation.28 | convolution fusion | flops 402653184 | bytes 7536640 | tf_op jit(solution)/shard_map/njcd,jdf->njcf/dot_general | solution.py:76
  205.8 1.0 fusion.57
  206.8 0.7 slice-done.7
  207.5 1.2 fusion.21
  208.8 25.8 %all_to_all.32 = f32[8,2,8,4096]{3,2,1,0:T(8,128)} all-to-all(f32[8,2,8,4096]{3,2,1,0:T(8,128)S(1)} %copy.109), channel_id=1, replica_groups=mesh['replica'=4,'expert'=8,'tensor'=4] {'expert'}, dimensions={0} | all-to-all | bytes 4194304 | tf_op jit(solution)/shard_map/all_to_all | solution.py:84
  235.3 0.2 select_reduce_fusion.1
  235.8 26.7 %reduce-scatter.6.cloned.1.call-done = f32[8,2,8,1024]{3,2,1,0:T(8,128)} async-done(((f32[8,2,8,4096]{3,2,1,0:T(8,128)}), f32[8,2,8,1024]{3,2,1,0:T(8,128)}) %reduce-scatter.6.cloned.1.call-update) | async-done | bytes 524304 | tf_op jit(solution)/shard_map/reduce_scatter | solution.py:85
  262.5 1.1 convert_element_type.88
  263.6 0.2 convolution_add_fusion
  263.8 12.3 %all_gather.35 = f32[16,4096]{1,0:T(8,128)S(1)} all-gather(f32[16,1024]{1,0:T(8,128)S(1)} %convolution_add_fusion), channel_id=1, replica_groups=mesh['replica'=4,'expert'=8,'tensor'=4] {'tensor'}, dimensions={1}, use_global_device_ids=true | all-gather | bytes 327680 | tf_op jit(solution)/shard_map/all_gather | solution.py:69
  276.3 0.5 convolution_convert_fusion
  276.7 17.7 %all_to_all.33 = bf16[8,2,8,4096]{3,2,1,0:T(8,128)(2,1)S(1)} all-to-all(bf16[8,2,8,4096]{3,2,1,0:T(8,128)(2,1)S(1)} %bitcast.141), channel_id=1, replica_groups=mesh['replica'=4,'expert'=8,'tensor'=4] {'expert'}, dimensions={0} | all-to-all | bytes 2097152 | tf_op jit(solution)/shard_map/all_to_all | solution.py:75
  294.5 4.0 %fusion.33 = f32[8,2,8,384]{3,2,0,1:T(8,128)S(1)} fusion(bf16[2,4096,384]{2,1,0:T(8,128)(2,1)} %add_convert_fusion.1, bf16[8,2,8,4096]{3,2,1,0:T(8,128)(2,1)S(1)} %all_to_all.33), kind=kOutput, calls=%fused_computation.29 | convolution fusion | flops 402653184 | bytes 7536640 | tf_op jit(solution)/shard_map/njcd,jdf->njcf/dot_general | solution.py:76
  298.5 1.0 fusion.60
  299.5 0.7 slice-done.9
  300.2 1.1 fusion.24
  301.5 25.7 %all_to_all.34 = f32[8,2,8,4096]{3,2,1,0:T(8,128)} all-to-all(f32[8,2,8,4096]{3,2,1,0:T(8,128)S(1)} %copy.116), channel_id=1, replica_groups=mesh['replica'=4,'expert'=8,'tensor'=4] {'expert'}, dimensions={0} | all-to-all | bytes 4194304 | tf_op jit(solution)/shard_map/all_to_all | solution.py:84
  327.6 27.6 %reduce-scatter.8.cloned.1.call-done = f32[8,2,8,1024]{3,2,1,0:T(8,128)} async-done(((f32[8,2,8,4096]{3,2,1,0:T(8,128)}), f32[8,2,8,1024]{3,2,1,0:T(8,128)}) %reduce-scatter.8.cloned.1.call-update) | async-done | bytes 524304 | tf_op jit(solution)/shard_map/reduce_scatter | solution.py:85
  355.2 1.1 convert_element_type.93
  356.3 0.9 fusion.85
  (98 shorter events, 3.8 us)
Async XLA Ops:
  24.5 77.5 %all-to-all-start = ((bf16[8,2,8,4096]{3,2,1,0:T(8,128)(2,1)}), bf16[8,2,8,4096]{3,2,1,0:T(8,128)(2,1)S(1)}, u32[]{:S(2)}, u32[]{:S(2)}) async-start(bf16[8,2,8,4096]{3,2,1,0:T(8,128)(2,1)} %bitcast.7), calls=%async_computation | async-start | bytes 2097152 | tf_op jit(solution)/shard_map/all_to_all | solution.py:75
  30.3 139.3 %reduce-scatter.4.cloned.1.call-start = ((), (), s32[]{:S(2)}) async-start(), calls=%async_computation.9 | async-start | bytes 2621440 | tf_op jit(solution)/shard_map/reduce_scatter | solution.py:85
  60.9 16.6 %slice-start = ((s8[6291456]{0:T(1024)(128)(4,1)}), s8[4194304]{0:T(1024)(128)(4,1)S(1)}, s32[]{:S(2)}) async-start(s8[6291456]{0:T(1024)(128)(4,1)} %bitcast.126), calls=%async_computation.12 | async-start | bytes 8388608
  70.0 7.5 %slice-start.1 = ((s8[6291456]{0:T(1024)(128)(4,1)}), s8[2097152]{0:T(1024)(128)(4,1)S(1)}, s32[]{:S(2)}) async-start(s8[6291456]{0:T(1024)(128)(4,1)} %bitcast.126), calls=%async_computation.13 | async-start | bytes 4194304
  70.0 27.5 %slice-start.2 = ((s8[6291456]{0:T(1024)(128)(4,1)}), s8[4194304]{0:T(1024)(128)(4,1)S(1)}, s32[]{:S(2)}) async-start(s8[6291456]{0:T(1024)(128)(4,1)} %bitcast.128), calls=%async_computation.14 | async-start | bytes 8388608
  77.4 4.5 %copy-start.4 = (bf16[2,8,384]{2,1,0:T(8,128)(2,1)S(1)}, bf16[2,8,384]{2,1,0:T(8,128)(2,1)}, u32[]{:S(2)}) copy-start(bf16[2,8,384]{2,1,0:T(8,128)(2,1)} %param.21) | copy-start | bytes 36868
  77.4 11.3 %copy-start.1 = (bf16[2,8,4096]{2,1,0:T(8,128)(2,1)S(1)}, bf16[2,8,4096]{2,1,0:T(8,128)(2,1)}, u32[]{:S(2)}) copy-start(bf16[2,8,4096]{2,1,0:T(8,128)(2,1)} %param.20) | copy-start | bytes 393220
  77.4 20.0 %slice-start.3 = ((s8[6291456]{0:T(1024)(128)(4,1)}), s8[2097152]{0:T(1024)(128)(4,1)S(1)}, s32[]{:S(2)}) async-start(s8[6291456]{0:T(1024)(128)(4,1)} %bitcast.128), calls=%async_computation.15 | async-start | bytes 4194304
  102.0 7.9 %slice-start.4 = ((s8[6291456]{0:T(1024)(128)(4,1)}), s8[4194304]{0:T(1024)(128)(4,1)S(1)}, s32[]{:S(2)}) async-start(s8[6291456]{0:T(1024)(128)(4,1)} %bitcast.130), calls=%async_computation.16 | async-start | bytes 8388608
  105.9 4.0 %slice-start.5 = ((s8[6291456]{0:T(1024)(128)(4,1)}), s8[2097152]{0:T(1024)(128)(4,1)S(1)}, s32[]{:S(2)}) async-start(s8[6291456]{0:T(1024)(128)(4,1)} %bitcast.130), calls=%async_computation.17 | async-start | bytes 4194304
  111.1 33.2 %copy-start.3 = (f32[3,16,4]{1,2,0:T(4,128)S(1)}, f32[3,16,4]{1,2,0:T(4,128)}, u32[]{:S(2)}) copy-start(f32[3,16,4]{1,2,0:T(4,128)} %param.16) | copy-start | bytes 2308
  111.1 59.6 %copy-start.2 = (bf16[16,1024]{1,0:T(8,128)(2,1)S(1)}, bf16[16,1024]{1,0:T(8,128)(2,1)}, u32[]{:S(2)}) copy-start(bf16[16,1024]{1,0:T(8,128)(2,1)} %param.13) | copy-start | bytes 98308
  111.1 72.3 %copy-start = (f32[4096]{0:T(1024)S(1)}, f32[4096]{0:T(1024)}, u32[]{:S(2)}) copy-start(f32[4096]{0:T(1024)} %param.14) | copy-start | bytes 49156
  143.1 119.4 %reduce-scatter.6.cloned.1.call-start = ((), (), s32[]{:S(2)}) async-start(), calls=%async_computation.10 | async-start | bytes 2621440 | tf_op jit(solution)/shard_map/reduce_scatter | solution.py:85
  183.9 21.8 %slice-start.10 = ((s8[6291456]{0:T(1024)(128)(4,1)}), s8[4194304]{0:T(1024)(128)(4,1)S(1)}, s32[]{:S(2)}) async-start(s8[6291456]{0:T(1024)(128)(4,1)} %bitcast.136), calls=%async_computation.22 | async-start | bytes 8388608
  201.7 4.0 %slice-start.11 = ((s8[6291456]{0:T(1024)(128)(4,1)}), s8[2097152]{0:T(1024)(128)(4,1)S(1)}, s32[]{:S(2)}) async-start(s8[6291456]{0:T(1024)(128)(4,1)} %bitcast.136), calls=%async_computation.23 | async-start | bytes 4194304
  201.7 5.0 %slice-start.6 = ((s8[6291456]{0:T(1024)(128)(4,1)}), s8[4194304]{0:T(1024)(128)(4,1)S(1)}, s32[]{:S(2)}) async-start(s8[6291456]{0:T(1024)(128)(4,1)} %bitcast.132), calls=%async_computation.18 | async-start | bytes 8388608
  205.7 1.8 slice-start.7
  234.6 120.6 %reduce-scatter.8.cloned.1.call-start = ((), (), s32[]{:S(2)}) async-start(), calls=%async_computation.11 | async-start | bytes 2621440 | tf_op jit(solution)/shard_map/reduce_scatter | solution.py:85
  276.2 22.2 %slice-start.12 = ((s8[6291456]{0:T(1024)(128)(4,1)}), s8[4194304]{0:T(1024)(128)(4,1)S(1)}, s32[]{:S(2)}) async-start(s8[6291456]{0:T(1024)(128)(4,1)} %bitcast.138), calls=%async_computation.24 | async-start | bytes 8388608
  294.5 4.0 %slice-start.13 = ((s8[6291456]{0:T(1024)(128)(4,1)}), s8[2097152]{0:T(1024)(128)(4,1)S(1)}, s32[]{:S(2)}) async-start(s8[6291456]{0:T(1024)(128)(4,1)} %bitcast.138), calls=%async_computation.25 | async-start | bytes 4194304
  294.5 5.0 %slice-start.8 = ((s8[6291456]{0:T(1024)(128)(4,1)}), s8[4194304]{0:T(1024)(128)(4,1)S(1)}, s32[]{:S(2)}) async-start(s8[6291456]{0:T(1024)(128)(4,1)} %bitcast.134), calls=%async_computation.20 | async-start | bytes 8388608
  298.4 1.8 slice-start.9
Sparse Core Ops, SparseCore 0:
  143.2 26.3 reduce-scatter.3
  234.7 27.7 reduce-scatter.5
  327.4 27.7 reduce-scatter.7
where the time goes:
time: 365 us; the launch traced here: 364 us
  blocking collectives  211 us (58%)
  waiting for transfers between devices  79.4 us (22%)
  matrix products  42.3 us (12%)
  between operations  14.2 us (4%)
  starting transfers between devices  6.12 us (2%)
  other arithmetic  6.1 us (2%)
  local copies, waits for them, and re-layouts  4.37 us (1%)
    all_to_all x3, blocking collectives, per_device(): lax.all_to_all(partial_value, 'expert', split_axis=0, concat_axis=0, tile...  83.3 us
    reduce_scatter x3, waiting for transfers between devices, per_device(): lax.psum_scatter(returned, 'tensor', scatter_dimension=3, tiled=True)  79.3 us
    all_gather x3, blocking collectives, per_device(): whole = lax.all_gather(current, 'tensor', axis=1, tiled=True)  37.3 us
    all_to_all x2, blocking collectives, per_device(): lax.all_to_all(outgoing, 'expert', split_axis=0, concat_axis=0, tiled=True)  35.5 us
    all_gather x1, blocking collectives, per_device(): lax.all_gather(up_a, 'replica', axis=1, tiled=True)  16.6 us
    dot_general x3, matrix products, merge_weight(): delta = jnp.einsum(form, left, right, preferred_element_type=jnp.float32)  16.4 us
    dot_general x3, matrix products, per_device(): jnp.einsum('njcd,jdf->njcf', arrived, merged_gate, preferred_element_type...  11.9 us
    all_gather x1, blocking collectives, per_device(): lax.all_gather(down_b, 'replica', axis=1, tiled=True)  9.11 us
  transfers between devices with their start and end apart: 4, of which 3 were waited for; matrix products, arithmetic and copies ran while one was open for 5% of the time, Pallas kernels for 0%

commit v1 on v0

v1 whole, which is shorter than its diff:
```python
import jax
import jax.numpy as jnp
from jax import lax
from jax.experimental import pallas as pl
from jax.experimental.pallas import tpu as pltpu
from jax.sharding import PartitionSpec as P

EPS = 1e-06
MESH = pl.DeviceIdType.MESH
BF = jnp.bfloat16
F32 = jnp.float32
NT = (((1,), (1,)), ((), ()))
ORDER = (2, 1, 3, 0)


def kernel(
    states, gain, ids, weights, ga, gb, ua, ub, da, db, gw, uw, dw,
    out_state, out_update,
    w, wd, abuf, sbuf, bd, adt, mixb, mixs, cur, upd, gs, gi, xb, acc, uacc, ssq, hbuf, vbuf, po, rb, s2, r2,
    wsem, ad_s, ad_r, mx_s, mx_r, a1s, a1r, a2s, a2r, b1s, b1r, b2s, b2r,
):
    r, e, t = lax.axis_index("replica"), lax.axis_index("expert"), lax.axis_index("tensor")
    y, z = e // 2, e % 2
    core = r % 2
    half = r // 2
    far = r + 2 - 4 * half
    other = r + 1 - 2 * core
    across = r + core * (2 - 4 * half)

    def dev(dt=0, dy=0, dz=0):
        return (across if dz else r, (y + dy) % 4 * 2 + (1 - z if dz else z), (t + dt) % 4)

    def peer(h, d, dz=0):
        return dev(dt=d, dz=dz) if h == 0 else dev(dy=d, dz=dz)

    def remote(src, dst, ss, rs, to):
        return pltpu.make_async_remote_copy(
            src_ref=src, dst_ref=dst, send_sem=ss, recv_sem=rs, device_id=to, device_id_type=MESH
        )

    loads = []
    for j in range(2):
        for m, ref in enumerate((gw, uw)):
            loads.append((ref.at[j], w.at[:, pl.ds(j * 768 + m * 384, 384)]))
    for j in range(2):
        loads.append((dw.at[j], wd.at[pl.ds(j * 384, 384)]))
    loads = [pltpu.make_async_copy(a, b, wsem.at[i]) for i, (a, b) in enumerate(loads)]
    for copy in loads:
        copy.start()

    plane = [(d, dz) for d in range(4) for dz in range(2) if (d, dz) != (0, 0)]
    everyone = [peer(0, d, dz) for d, dz in plane] + [peer(1, d, dz) for d, dz in plane if d]
    everyone += [(far, e, t), (other, e, t)]
    barrier = pltpu.get_barrier_semaphore()
    for to in everyone:
        pl.semaphore_signal(barrier, inc=1, device_id=to, device_id_type=MESH)

    cur[...] = states[...].astype(F32)
    for c in range(8):
        row = jnp.concatenate([gain[pl.ds(4 * c + i, 1), :] for i in range(4)], axis=1)
        gs[c] = row
        gi[c] = 1.0 / row
    lane = lax.broadcasted_iota(jnp.int32, (16, 128), 1)
    mix = jnp.zeros((16, 128), F32)
    for s in range(3):
        raw = weights[s]
        raw = raw / jnp.sum(raw, axis=1, keepdims=True)
        chosen = ids[s]
        for k in range(4):
            mix = mix + jnp.where(lane == chosen[:, k : k + 1] + 16 * s, raw[:, k : k + 1], 0.0)
    mixb[y, z] = mix

    def pack(ref, scale):
        return (jnp.concatenate([ref[0].astype(F32), ref[1].astype(F32)], axis=0) * scale).astype(BF)

    abuf[r, 0] = pack(ga, 1.0)
    abuf[r, 1] = pack(ua, 1.0)
    sbuf[r, 0] = pack(gb, 2.0)
    sbuf[r, 1] = pack(ub, 2.0)
    sbuf[r, 2] = pack(da, 1.0)
    wd[pl.ds(pl.multiple_of(768 + 16 * r, 16), 16), :] = pack(db, 2.0)

    pl.semaphore_wait(barrier, len(everyone))

    def ranks(q, kind, to):
        rows = wd.at[pl.ds(pl.multiple_of(768 + 16 * q, 16), 16)]
        refs = (abuf.at[q], sbuf.at[q], rows)
        return [remote(x, x, ad_s.at[kind, i], ad_r.at[kind, i], to) for i, x in enumerate(refs)]

    to_far = ranks(r, 0, (far, e, t))
    to_other = ranks(r, 1, (other, e, t))
    passed_on = ranks(far, 2, (other, e, t))
    mixes = [
        remote(mixb.at[y, z], mixb.at[y, z], mx_s.at[2 * d + dz], mx_r.at[2 * d + dz], peer(1, d, dz)) for d, dz in plane
    ]

    def step(s, carry):
        for h in range(2):
            cols = slice(h * 512, h * 512 + 512)
            xb[h, t, y, z] = (cur[:, cols] * gs[2 * t + h]).astype(BF)
        first = {}
        for d, dz in sorted(plane, key=lambda p: -p[1]):
            for h in range(2):
                block = xb.at[h, t, y, z]
                i = 2 * d + dz
                first[h, d, dz] = remote(block, block, a1s.at[h, i], a1r.at[h, i], peer(h, d, dz))
                first[h, d, dz].start()

        @pl.when(s == 0)
        def _():
            for copy in mixes + to_far + to_other:
                copy.start()

        second = {}
        for d in range(4):
            for h in range(2):
                for dz in range(2):
                    if (d, dz) != (0, 0):
                        first[h, d, dz].wait_recv()
                block = xb.at[0, (t - d + 4) % 4, y] if h == 0 else xb.at[1, t, (y - d + 4) % 4]
                for p in ORDER[:3]:
                    second[h, d, p] = remote(block, block, a2s.at[h, d, p], a2r.at[h, d, p], peer(1 - h, p))
                    second[h, d, p].start()

        @pl.when(s == 0)
        def _():
            for copy in loads:
                copy.wait()

        acc[...] = jnp.zeros_like(acc)
        ssq[...] = jnp.zeros_like(ssq)

        def chunk(h, tc):
            x = xb[h, tc].reshape(128, 512)
            k0 = pl.multiple_of(tc * 1024 + h * 512, 512)
            for n in range(3):
                cols = slice(n * 512, n * 512 + 512)
                acc[:, cols] += jnp.dot(x, w[pl.ds(k0, 512), cols], preferred_element_type=F32)
            plain = x.astype(F32) * gi[2 * tc + h]
            plain = plain * plain
            ssq[...] += plain[:, :128] + plain[:, 128:256] + plain[:, 256:384] + plain[:, 384:]

        chunk(1, t)
        for d in range(4):
            for p in range(1, 4):
                second[0, d, p].wait_recv()
            chunk(0, (t - d + 4) % 4)
        for p in ORDER[:3]:
            for d in range(4):
                second[1, d, p].wait_recv()
            chunk(1, (t - p + 4) % 4)

        @pl.when(s == 0)
        def _():
            for copy in to_far:
                copy.wait_recv()
            for copy in passed_on:
                copy.start()
            for copy in to_other + passed_on + mixes:
                copy.wait_recv()
            bd[...] = jnp.zeros_like(bd)
            for q in range(4):
                for j in range(2):
                    keep = lax.broadcasted_iota(jnp.int32, (16, 384), 0) // 8 == j
                    for m in range(2):
                        part = jnp.where(keep, sbuf[q, m].astype(F32), 0.0).astype(BF)
                        bd[q * 32 + m * 16 : q * 32 + m * 16 + 16, j * 768 + m * 384 : j * 768 + m * 384 + 384] = part
                    part = jnp.where(keep, sbuf[q, 2].astype(F32), 0.0).astype(BF)
                    adt[q * 16 : q * 16 + 16, j * 384 : j * 384 + 384] = part
            for copy in to_far + to_other + passed_on + mixes:
                copy.wait_send()

        uacc[...] = jnp.zeros_like(uacc)
        for tc in range(4):
            for h in range(2):
                k0 = tc * 1024 + h * 512
                a = abuf[:, :, :, k0 : k0 + 512].reshape(128, 512)
                uacc[...] += lax.dot_general(xb[h, tc].reshape(128, 512), a, NT, preferred_element_type=F32)
        low = uacc[...].astype(BF)
        scale = lax.rsqrt(jnp.sum(ssq[...], axis=1, keepdims=True) * (1.0 / 4096.0) + EPS)
        mixed = mixb[...].reshape(128, 128)
        lanes = lax.broadcasted_iota(jnp.int32, (128, 128), 1)
        for j in range(2):
            here = jnp.sum(jnp.where(lanes == s * 16 + 2 * e + j, mixed, 0.0), axis=1, keepdims=True)
            for n in range(3):
                g0 = j * 768 + n * 128
                u0 = g0 + 384
                gate = acc[:, g0 : g0 + 128] + jnp.dot(low, bd[:, g0 : g0 + 128], preferred_element_type=F32)
                upper = acc[:, u0 : u0 + 128] + jnp.dot(low, bd[:, u0 : u0 + 128], preferred_element_type=F32)
                gate, upper = gate * scale, upper * scale
                hidden = gate / (1.0 + jnp.exp(-gate)) * upper * here
                hbuf[:, j * 384 + n * 128 : j * 384 + n * 128 + 128] = hidden.astype(BF)
        vbuf[...] = lax.dot_general(hbuf[...], adt[...], NT, preferred_element_type=F32).astype(BF)

        third = {}
        for d in ORDER:
            tc = (t + d) % 4
            for h in (1, 0):
                k0 = pl.multiple_of(tc * 1024 + h * 512, 512)
                part = jnp.dot(hbuf[...], wd[0:768, pl.ds(k0, 512)], preferred_element_type=F32)
                part = part + jnp.dot(vbuf[...], wd[768:832, pl.ds(k0, 512)], preferred_element_type=F32)
                po[h, tc] = part.astype(BF).reshape(4, 2, 16, 512)
                if h == 0:
                    for p in ORDER[:3]:
                        third[0, d, p] = remote(
                            po.at[0, tc, (y + p) % 4], rb.at[0, p - 1, tc], b1s.at[0, d, p], b1r.at[0, d, p], peer(1, p)
                        )
                        third[0, d, p].start()
                elif d:
                    for i in ORDER:
                        ys = (y + i) % 4
                        third[1, i, d] = remote(
                            po.at[1, tc, ys], rb.at[1, d - 1, ys], b1s.at[1, i, d], b1r.at[1, i, d], peer(0, d)
                        )
                        third[1, i, d].start()
        for copy in list(first.values()) + list(second.values()):
            copy.wait_send()
        fourth = {}
        for d in ORDER:
            for h in range(2):
                for p in ORDER[:3]:
                    third[h, d, p].wait_recv()
                i = (t + d) % 4 if h == 0 else (y + d) % 4
                for dz in range(2):
                    zz = 1 - z if dz else z
                    own = po[0, i, y, zz] if h == 0 else po[1, t, i, zz]
                    total = own.astype(F32)
                    for p in range(3):
                        total = total + rb[h, p, i, zz].astype(F32)
                    if (d, dz) == (0, 0):
                        upd[:, h * 512 : h * 512 + 512] = total
                    else:
                        n = 2 * d + dz
                        s2[h, n] = total.astype(BF)
                        fourth[h, d, dz] = remote(s2.at[h, n], r2.at[h, n], b2s.at[h, n], b2r.at[h, n], peer(h, d, dz))
                        fourth[h, d, dz].start()
        for copy in third.values():
            copy.wait_send()
        for h in range(2):
            cols = slice(h * 512, h * 512 + 512)
            total = upd[:, cols]
            for d, dz in plane:
                fourth[h, d, dz].wait_recv()
                total = total + r2[h, 2 * d + dz].astype(F32)
            upd[:, cols] = total
            cur[:, cols] += total
        for copy in fourth.values():
            copy.wait_send()
        return carry

    lax.fori_loop(0, 3, step, 0)
    out_state[...] = cur[...]
    out_update[...] = upd[...]


def per_device(states, gain, ids, weights, gw, uw, dw, ga, gb, ua, ub, da, db):
    vmem = pl.BlockSpec(memory_space=pltpu.VMEM)
    hbm = pl.BlockSpec(memory_space=pl.ANY)
    dma = pltpu.SemaphoreType.DMA
    scratch = [
        pltpu.VMEM((4096, 1536), BF),
        pltpu.VMEM((832, 4096), BF),
        pltpu.VMEM((4, 2, 16, 4096), BF),
        pltpu.VMEM((4, 3, 16, 384), BF),
        pltpu.VMEM((128, 1536), BF),
        pltpu.VMEM((64, 768), BF),
        pltpu.VMEM((4, 2, 16, 128), F32),
        pltpu.VMEM((8, 128), F32),
        pltpu.VMEM((16, 1024), F32),
        pltpu.VMEM((16, 1024), F32),
        pltpu.VMEM((8, 1, 512), F32),
        pltpu.VMEM((8, 1, 512), F32),
        pltpu.VMEM((2, 4, 4, 2, 16, 512), BF),
        pltpu.VMEM((128, 1536), F32),
        pltpu.VMEM((128, 128), F32),
        pltpu.VMEM((128, 128), F32),
        pltpu.VMEM((128, 768), BF),
        pltpu.VMEM((128, 64), BF),
        pltpu.VMEM((2, 4, 4, 2, 16, 512), BF),
        pltpu.VMEM((2, 3, 4, 2, 16, 512), BF),
        pltpu.VMEM((2, 8, 16, 512), BF),
        pltpu.VMEM((2, 8, 16, 512), BF),
        dma((6,)),
        dma((3, 3)),
        dma((3, 3)),
        dma((8,)),
        dma((8,)),
        dma((2, 8)),
        dma((2, 8)),
        dma((2, 4, 4)),
        dma((2, 4, 4)),
        dma((2, 4, 4)),
        dma((2, 4, 4)),
        dma((2, 8)),
        dma((2, 8)),
    ]
    shape = jax.ShapeDtypeStruct((16, 1024), F32)
    return pl.pallas_call(
        kernel,
        out_shape=(shape, shape),
        in_specs=[vmem] * 10 + [hbm] * 3,
        out_specs=(vmem, vmem),
        scratch_shapes=scratch,
        compiler_params=pltpu.CompilerParams(collective_id=0, has_side_effects=True, vmem_limit_bytes=50 << 20),
    )(states, gain.reshape(32, 128), ids, weights, ga, gb, ua, ub, da, db, gw, uw, dw)


def solution(mesh):
    return jax.shard_map(
        per_device,
        mesh=mesh,
        in_specs=(
            P(("replica", "expert"), "tensor"),
            P(),
            P(None, ("replica", "expert"), None),
            P(None, ("replica", "expert"), None),
            P("expert", None, "tensor"),
            P("expert", None, "tensor"),
            P("expert", "tensor", None),
            P("expert", "replica", None),
            P("expert", "replica", "tensor"),
            P("expert", "replica", None),
            P("expert", "replica", "tensor"),
            P("expert", "replica", "tensor"),
            P("expert", "replica", None),
        ),
        out_specs=(P(("replica", "expert"), "tensor"), P(("replica", "expert"), "tensor")),
        check_vma=False,
    )
```

time: 365 us -> 101 us (0.28)
  the two profiles are of different devices: /device:TPU:0 before, /device:TPU:64 now
where the time goes in v1:
time: 101 us; the launch traced here: 100 us
  Pallas kernels  90.3 us (89%)
  local copies, waits for them, and re-layouts  9.12 us (9%)
    pallas_call x1, Pallas kernels, per_device(): pl.pallas_call(kernel, out_shape=(shape, shape), in_specs=[vmem] * 10 + [...  90.3 us
    unnamed x20, local copies, waits for them, and re-layouts  9.12 us

profile of v1, /device:TPU:64, one launch (start us, length us, event | category | flops | bytes accessed | tf_op | source)
XLA Modules:
  0.0 100.1 jit_solution(11063525012491989301)
XLA Ops:
  0.6 0.8 copy.15.ids
  1.4 0.8 copy.16.weights
  2.2 0.0 copy-start
  2.2 0.9 copy-done
  3.1 0.0 copy-start.1
  3.1 0.9 copy-done.1
  4.0 0.0 copy-start.2
  4.0 0.9 copy-done.2
  4.9 0.0 copy-start.3
  4.9 0.8 copy-done.3
  5.7 0.0 copy-start.4
  5.7 0.7 copy-done.4
  6.4 0.0 copy-start.5
  6.4 0.7 copy-done.5
  7.1 0.0 copy-start.6
  7.1 0.7 copy-done.6
  7.8 0.0 copy-start.7
  7.8 0.7 copy-done.7
  8.5 90.3 %shard_map.140 = (f32[16,1024]{1,0:T(8,128)S(1)}, f32[16,1024]{1,0:T(8,128)S(1)}) custom-call(bf16[16,1024]{1,0:T(8,128)(2,1)S(1)} %copy-done.3, f32[32,128]{1,0:T(8,128)S(1)} %bitcast.1, s32[3,16,4]{2,1,0:T(8,128)S(1)} %copy.15.ids, f32[3,16,4]{2,1,0:T(8,128)S(1)} %copy.16.weights, bf16[2,8,4096]{2,1,0:T(8,128)(2,1)S(1)} %copy-done, ...), custom_call_target="tpu_custom_call" | custom-call | tf_op jit(solution)/shard_map/pallas_call | solution.py:298
  98.8 0.6 copy.19
  99.4 0.6 copy.20
Async XLA Ops:
  2.2 0.9 copy-start
  3.1 0.9 copy-start.1
  4.0 0.9 copy-start.2
  4.9 0.8 copy-start.3
  5.7 0.7 copy-start.4
  6.4 0.7 copy-start.5
  7.1 0.7 copy-start.6
  7.8 0.7 copy-start.7

commit v2 on v1

v2 whole, which is shorter than its diff:
```python
import jax
import jax.numpy as jnp
from jax import lax
from jax.experimental import pallas as pl
from jax.experimental.pallas import tpu as pltpu
from jax.sharding import PartitionSpec as P

EPS = 1e-06
MESH = pl.DeviceIdType.MESH
BF = jnp.bfloat16
F32 = jnp.float32
NT = (((1,), (1,)), ((), ()))
ORDER = (2, 1, 3, 0)


def kernel(
    states_in, gain_in, ids_in, weights_in, ga_in, gb_in, ua_in, ub_in, da_in, db_in, gw, uw, dw,
    out_state, out_update,
    states, gain, ids, weights, ga, gb, ua, ub, da, db,
    w, wd, abuf, sbuf, bd, adt, mixb, mixs, cur, upd, gs, gi, xb, acc, uacc, ssq, hbuf, vbuf, po, rb, s2, r2,
    isem, wsem, ad_s, ad_r, mx_s, mx_r, a1s, a1r, a2s, a2r, b1s, b1r, b2s, b2r,
):
    r, e, t = lax.axis_index("replica"), lax.axis_index("expert"), lax.axis_index("tensor")
    y, z = e // 2, e % 2
    core = r % 2
    half = r // 2
    far = r + 2 - 4 * half
    other = r + 1 - 2 * core
    across = r + core * (2 - 4 * half)

    ts = [t] + [(t + d) % 4 for d in range(1, 4)]
    ys = [y] + [(y + d) % 4 for d in range(1, 4)]
    zs = (z, 1 - z)

    def dev(dt=0, dy=0, dz=0):
        return (across if dz else r, ys[dy] * 2 + zs[dz], ts[dt])

    def peer(h, d, dz=0):
        return dev(dt=d, dz=dz) if h == 0 else dev(dy=d, dz=dz)

    def remote(src, dst, ss, rs, to):
        return pltpu.make_async_remote_copy(
            src_ref=src, dst_ref=dst, send_sem=ss, recv_sem=rs, device_id=to, device_id_type=MESH
        )

    plane = [(d, dz) for d in range(4) for dz in range(2) if (d, dz) != (0, 0)]
    everyone = [peer(0, d, dz) for d, dz in plane] + [peer(1, d, dz) for d, dz in plane if d]
    everyone += [(far, e, t), (other, e, t)]
    barrier = pltpu.get_barrier_semaphore()
    for to in everyone:
        pl.semaphore_signal(barrier, inc=1, device_id=to, device_id_type=MESH)

    def await_bytes(like, sem):
        pltpu.make_async_copy(like, like, sem).wait()

    small = (
        (states_in, states), (gain_in, gain), (ids_in, ids), (weights_in, weights), (ga_in, ga),
        (ua_in, ua), (gb_in, gb), (ub_in, ub), (da_in, da), (db_in, db),
    )
    small = [pltpu.make_async_copy(a, b, isem.at[i]) for i, (a, b) in enumerate(small)]
    for copy in small:
        copy.start()
    loads = []
    for j in range(2):
        for m, ref in enumerate((gw, uw)):
            loads.append((ref.at[j], w.at[:, pl.ds(j * 768 + m * 384, 384)]))
    for j in range(2):
        loads.append((dw.at[j], wd.at[pl.ds(j * 384, 384)]))
    loads = [pltpu.make_async_copy(a, b, wsem.at[i]) for i, (a, b) in enumerate(loads)]
    for copy in loads:
        copy.start()

    for copy in small:
        copy.wait()

    cur[...] = states[...].astype(F32)
    for c in range(8):
        row = jnp.concatenate([gain[pl.ds(4 * c + i, 1), :] for i in range(4)], axis=1)
        gs[c] = row
        gi[c] = 1.0 / row
    rows = lax.broadcasted_iota(jnp.int32, (128, 16), 0)
    mix = jnp.zeros((128, 16), F32)
    for s in range(3):
        raw = weights[s]
        raw = raw / jnp.sum(raw, axis=0, keepdims=True)
        chosen = ids[s]
        for k in range(4):
            mix = mix + jnp.where(rows == chosen[k : k + 1, :] + 16 * s, raw[k : k + 1, :], 0.0)
    mixb[y, z] = mix.T

    def pack(ref, scale):
        return (jnp.concatenate([ref[0].astype(F32), ref[1].astype(F32)], axis=0) * scale).astype(BF)

    abuf[r, 0] = pack(ga, 1.0)
    abuf[r, 1] = pack(ua, 1.0)
    sbuf[r, 0] = pack(gb, 2.0)
    sbuf[r, 1] = pack(ub, 2.0)
    sbuf[r, 2] = pack(da, 1.0)
    wd[pl.ds(pl.multiple_of(768 + 16 * r, 16), 16), :] = pack(db, 2.0)

    pl.semaphore_wait(barrier, len(everyone))

    def ranks(q, kind, to):
        rows = wd.at[pl.ds(pl.multiple_of(768 + 16 * q, 16), 16)]
        refs = (abuf.at[q], sbuf.at[q], rows)
        return [remote(x, x, ad_s.at[kind, i], ad_r.at[kind, i], to) for i, x in enumerate(refs)]

    to_far = ranks(r, 0, (far, e, t))
    to_other = ranks(r, 1, (other, e, t))
    passed_on = ranks(far, 2, (other, e, t))
    mixes = [
        remote(mixb.at[y, z], mixb.at[y, z], mx_s.at[2 * d + dz], mx_r.at[2 * d + dz], peer(1, d, dz)) for d, dz in plane
    ]

    def step(s, carry):
        for h in range(2):
            cols = slice(h * 512, h * 512 + 512)
            xb[h, t, y, z] = (cur[:, cols] * gs[2 * t + h]).astype(BF)
        for d, dz in ((2, 1), (1, 1), (3, 1), (2, 0), (0, 1), (1, 0), (3, 0)):
            for h in range(2):
                block = xb.at[h, t, y, z]
                remote(block, block, a1s.at[h], a1r.at[h, d], peer(h, d, dz)).start()

        def onward(h, d, block):
            for p in ORDER[:3]:
                group = d if h == 0 else p
                remote(block, block, a2s.at[h], a2r.at[h, group], peer(1 - h, p)).start()

        for h in range(2):
            onward(h, 0, xb.at[h, t, y, z])

        @pl.when(s == 0)
        def _():
            for copy in to_far + to_other + mixes:
                copy.start()

        for d in (0, 1, 3, 2):
            for h in range(2):
                await_bytes(s2.at[0, pl.ds(0, 2 if d else 1)], a1r.at[h, d])
                if d:
                    onward(h, d, xb.at[0, ts[4 - d], y] if h == 0 else xb.at[1, t, ys[4 - d]])
                else:
                    onward(h, 0, xb.at[h, t, y, zs[1]])

        @pl.when(s == 0)
        def _():
            for copy in loads:
                copy.wait()

        acc[...] = jnp.zeros_like(acc)
        ssq[...] = jnp.zeros_like(ssq)
        uacc[...] = jnp.zeros_like(uacc)

        def low_rank(h, tc, x):
            a = abuf[:, :, :, pl.ds(pl.multiple_of(tc * 1024 + h * 512, 512), 512)].reshape(128, 512)
            uacc[...] += lax.dot_general(x, a, NT, preferred_element_type=F32)

        def chunk(h, tc):
            x = xb[h, tc].reshape(128, 512)
            k0 = pl.multiple_of(tc * 1024 + h * 512, 512)
            for n in range(3):
                cols = slice(n * 512, n * 512 + 512)
                acc[:, cols] += jnp.dot(x, w[pl.ds(k0, 512), cols], preferred_element_type=F32)
            plain = x.astype(F32) * gi[2 * tc + h]
            plain = plain * plain
            ssq[...] += plain[:, :128] + plain[:, 128:256] + plain[:, 256:384] + plain[:, 384:]

            @pl.when(s > 0)
            def _():
                low_rank(h, tc, x)

        chunk(1, t)
        for d, p in ((0, 0), (1, 0), (3, 2), (2, 1)):
            await_bytes(rb.at[0, :, 0], a2r.at[0, d])
            chunk(0, ts[(4 - d) % 4])
            if p:
                await_bytes(po.at[0, 0], a2r.at[1, p])
                chunk(1, ts[4 - p])
            if d == 1:

                @pl.when(s == 0)
                def _():
                    to_far[0].wait_recv()
                    passed_on[0].start()

        await_bytes(po.at[0, 0], a2r.at[1, 3])
        chunk(1, ts[1])

        @pl.when(s == 0)
        def _():
            for i in (1, 2):
                to_far[i].wait_recv()
                passed_on[i].start()
            for copy in to_other + passed_on + mixes:
                copy.wait_recv()
            bd[...] = jnp.zeros_like(bd)
            for q in range(4):
                for j in range(2):
                    keep = lax.broadcasted_iota(jnp.int32, (16, 384), 0) // 8 == j
                    for m in range(2):
                        part = jnp.where(keep, sbuf[q, m].astype(F32), 0.0).astype(BF)
                        bd[q * 32 + m * 16 : q * 32 + m * 16 + 16, j * 768 + m * 384 : j * 768 + m * 384 + 384] = part
                    part = jnp.where(keep, sbuf[q, 2].astype(F32), 0.0).astype(BF)
                    adt[q * 16 : q * 16 + 16, j * 384 : j * 384 + 384] = part
            for tc in range(4):
                for h in range(2):
                    low_rank(h, tc, xb[h, tc].reshape(128, 512))
            for copy in to_far + to_other + passed_on + mixes:
                copy.wait_send()

        low = uacc[...].astype(BF)
        scale = lax.rsqrt(jnp.sum(ssq[...], axis=1, keepdims=True) * (1.0 / 4096.0) + EPS)
        mixed = mixb[...].reshape(128, 128)
        lanes = lax.broadcasted_iota(jnp.int32, (128, 128), 1)
        for j in range(2):
            here = jnp.sum(jnp.where(lanes == s * 16 + 2 * e + j, mixed, 0.0), axis=1, keepdims=True)
            for n in range(3):
                g0 = j * 768 + n * 128
                u0 = g0 + 384
                gate = acc[:, g0 : g0 + 128] + jnp.dot(low, bd[:, g0 : g0 + 128], preferred_element_type=F32)
                upper = acc[:, u0 : u0 + 128] + jnp.dot(low, bd[:, u0 : u0 + 128], preferred_element_type=F32)
                gate, upper = gate * scale, upper * scale
                hidden = gate / (1.0 + jnp.exp(-gate)) * upper * here
                hbuf[:, j * 384 + n * 128 : j * 384 + n * 128 + 128] = hidden.astype(BF)
        vbuf[...] = lax.dot_general(hbuf[...], adt[...], NT, preferred_element_type=F32).astype(BF)

        for d in ORDER:
            tc = ts[d]
            for h in (1, 0):
                k0 = pl.multiple_of(tc * 1024 + h * 512, 512)
                part = jnp.dot(hbuf[...], wd[0:768, pl.ds(k0, 512)], preferred_element_type=F32)
                part = part + jnp.dot(vbuf[...], wd[768:832, pl.ds(k0, 512)], preferred_element_type=F32)
                po[h, tc] = part.astype(BF).reshape(4, 2, 16, 512)
                if h == 0:
                    for p in ORDER[:3]:
                        remote(po.at[0, tc, ys[p]], rb.at[0, p - 1, tc], b1s.at[0], b1r.at[0, d], peer(1, p)).start()
                elif d:
                    for i in ORDER:
                        remote(po.at[1, tc, ys[i]], rb.at[1, d - 1, ys[i]], b1s.at[1], b1r.at[1, i], peer(0, d)).start()
        for h in range(2):
            await_bytes(s2.at[0, pl.ds(0, 7)], a1s.at[h])
            await_bytes(po.at[0, pl.ds(0, 3)], a2s.at[h])
        for d in ORDER:
            for h in range(2):
                await_bytes(rb.at[0, :, 0], b1r.at[h, d])
                i = ts[d] if h == 0 else ys[d]
                for dz in range(2):
                    zz = zs[dz]
                    own = po[0, i, y, zz] if h == 0 else po[1, t, i, zz]
                    total = own.astype(F32)
                    for p in range(3):
                        total = total + rb[h, p, i, zz].astype(F32)
                    if (d, dz) == (0, 0):
                        upd[:, h * 512 : h * 512 + 512] = total
                    else:
                        n = 2 * d + dz
                        s2[h, n] = total.astype(BF)
                        remote(s2.at[h, n], r2.at[h, n], b2s.at[h], b2r.at[h], peer(h, d, dz)).start()
        for h in range(2):
            await_bytes(po.at[0, pl.ds(0, 3)], b1s.at[h])
        for h in range(2):
            cols = slice(h * 512, h * 512 + 512)
            total = upd[:, cols]
            await_bytes(s2.at[0, pl.ds(0, 7)], b2r.at[h])
            for d, dz in plane:
                total = total + r2[h, 2 * d + dz].astype(F32)
            upd[:, cols] = total
            cur[:, cols] += total
        for h in range(2):
            await_bytes(s2.at[0, pl.ds(0, 7)], b2s.at[h])
        return carry

    lax.fori_loop(0, 3, step, 0)
    out_state[...] = cur[...]
    out_update[...] = upd[...]


def per_device(states, gain, ids, weights, gw, uw, dw, ga, gb, ua, ub, da, db):
    vmem = pl.BlockSpec(memory_space=pltpu.VMEM)
    hbm = pl.BlockSpec(memory_space=pltpu.HBM)
    dma = pltpu.SemaphoreType.DMA
    args = (states, gain.reshape(32, 128), jnp.swapaxes(ids, 1, 2), jnp.swapaxes(weights, 1, 2), ga, gb, ua, ub, da, db, gw, uw, dw)
    scratch = [pltpu.VMEM(x.shape, x.dtype) for x in args[:10]] + [
        pltpu.VMEM((4096, 1536), BF),
        pltpu.VMEM((832, 4096), BF),
        pltpu.VMEM((4, 2, 16, 4096), BF),
        pltpu.VMEM((4, 3, 16, 384), BF),
        pltpu.VMEM((128, 1536), BF),
        pltpu.VMEM((64, 768), BF),
        pltpu.VMEM((4, 2, 16, 128), F32),
        pltpu.VMEM((8, 128), F32),
        pltpu.VMEM((16, 1024), F32),
        pltpu.VMEM((16, 1024), F32),
        pltpu.VMEM((8, 1, 512), F32),
        pltpu.VMEM((8, 1, 512), F32),
        pltpu.VMEM((2, 4, 4, 2, 16, 512), BF),
        pltpu.VMEM((128, 1536), F32),
        pltpu.VMEM((128, 128), F32),
        pltpu.VMEM((128, 128), F32),
        pltpu.VMEM((128, 768), BF),
        pltpu.VMEM((128, 64), BF),
        pltpu.VMEM((2, 4, 4, 2, 16, 512), BF),
        pltpu.VMEM((2, 3, 4, 2, 16, 512), BF),
        pltpu.VMEM((2, 8, 16, 512), BF),
        pltpu.VMEM((2, 8, 16, 512), BF),
        dma((10,)),
        dma((6,)),
        dma((3, 3)),
        dma((3, 3)),
        dma((8,)),
        dma((8,)),
        dma((2,)),
        dma((2, 4)),
        dma((2,)),
        dma((2, 4)),
        dma((2,)),
        dma((2, 4)),
        dma((2,)),
        dma((2,)),
    ]
    shape = jax.ShapeDtypeStruct((16, 1024), F32)
    return pl.pallas_call(
        kernel,
        out_shape=(shape, shape),
        in_specs=[hbm] * 13,
        out_specs=(vmem, vmem),
        scratch_shapes=scratch,
        compiler_params=pltpu.CompilerParams(collective_id=0, has_side_effects=True, vmem_limit_bytes=62 << 20),
    )(*args)


def solution(mesh):
    return jax.shard_map(
        per_device,
        mesh=mesh,
        in_specs=(
            P(("replica", "expert"), "tensor"),
            P(),
            P(None, ("replica", "expert"), None),
            P(None, ("replica", "expert"), None),
            P("expert", None, "tensor"),
            P("expert", None, "tensor"),
            P("expert", "tensor", None),
            P("expert", "replica", None),
            P("expert", "replica", "tensor"),
            P("expert", "replica", None),
            P("expert", "replica", "tensor"),
            P("expert", "replica", "tensor"),
            P("expert", "replica", None),
        ),
        out_specs=(P(("replica", "expert"), "tensor"), P(("replica", "expert"), "tensor")),
        check_vma=False,
    )
```

time: 101 us -> 92.4 us (0.915)
  the two profiles are of different devices: /device:TPU:64 before, /device:TPU:0 now
where the time goes in v2:
time: 92.4 us; the launch traced here: 91.9 us
  Pallas kernels  88.3 us (96%)
  local copies, waits for them, and re-layouts  2.95 us (3%)
    pallas_call x1, Pallas kernels, per_device(): pl.pallas_call(kernel, out_shape=(shape, shape), in_specs=[hbm] * 13, out...  88.3 us
    unnamed x2, local copies, waits for them, and re-layouts  2.95 us

profile of v2, /device:TPU:0, one launch (start us, length us, event | category | flops | bytes accessed | tf_op | source)
XLA Modules:
  0.0 91.9 jit_solution(15369971380934679740)
XLA Ops:
  0.6 88.3 %shard_map.140 = (f32[16,1024]{1,0:T(8,128)}, f32[16,1024]{1,0:T(8,128)}) custom-call(bf16[16,1024]{1,0:T(8,128)(2,1)} %states_in.1, f32[32,128]{1,0:T(8,128)} %bitcast.3, s32[3,4,16]{2,1,0:T(4,128)} %bitcast.4, f32[3,4,16]{2,1,0:T(4,128)} %bitcast.5, bf16[2,8,4096]{2,1,0:T(8,128)(2,1)} %ga_in.1, bf16[2,8,384]{2,1,0:T(8,128)(2,1)} %gb_in.1, ...), custom_call_target="tpu_custom_call" | custom-call | tf_op jit(solution)/shard_map/pallas_call | solution.py:322
  89.0 1.5 %copy.17 = f32[16,1024]{1,0:T(8,128)} copy(f32[16,1024]{1,0:T(8,128)} %get-tuple-element.4) | data formatting | bytes 131072
  90.4 1.5 %copy.18 = f32[16,1024]{1,0:T(8,128)} copy(f32[16,1024]{1,0:T(8,128)} %get-tuple-element.5) | data formatting | bytes 131072

commit v3 on v2

--- a/solution.py
+++ b/solution.py
@@ -17,7 +17,7 @@
     states_in, gain_in, ids_in, weights_in, ga_in, gb_in, ua_in, ub_in, da_in, db_in, gw, uw, dw,
     out_state, out_update,
     states, gain, ids, weights, ga, gb, ua, ub, da, db,
-    w, wd, abuf, sbuf, bd, adt, mixb, mixs, cur, upd, gs, gi, xb, acc, uacc, ssq, hbuf, vbuf, po, rb, s2, r2,
+    w, wd, abuf, sbuf, bd, adt, mixb, hs, cur, upd, gs, gi, xb, acc, uacc, ssq, hbuf, vbuf, po, rb, s2, r2,
     isem, wsem, ad_s, ad_r, mx_s, mx_r, a1s, a1r, a2s, a2r, b1s, b1r, b2s, b2r,
 ):
     r, e, t = lax.axis_index("replica"), lax.axis_index("expert"), lax.axis_index("tensor")
@@ -131,7 +131,7 @@
 
         @pl.when(s == 0)
         def _():
-            for copy in to_far + to_other + mixes:
+            for copy in mixes + to_far + to_other:
                 copy.start()
 
         for d in (0, 1, 3, 2):
@@ -141,6 +141,17 @@
                     onward(h, d, xb.at[0, ts[4 - d], y] if h == 0 else xb.at[1, t, ys[4 - d]])
                 else:
                     onward(h, 0, xb.at[h, t, y, zs[1]])
+
+        @pl.when(s == 0)
+        def _():
+            for copy in mixes:
+                copy.wait_recv()
+
+        mixed = mixb[...].reshape(128, 128)
+        lanes = lax.broadcasted_iota(jnp.int32, (128, 128), 1)
+        for j in range(2):
+            here = jnp.sum(jnp.where(lanes == s * 16 + 2 * e + j, mixed, 0.0), axis=1, keepdims=True)
+            hs[j] = jnp.broadcast_to(here, (128, 128))
 
         @pl.when(s == 0)
         def _():
@@ -188,10 +199,9 @@
 
         @pl.when(s == 0)
         def _():
-            for i in (1, 2):
-                to_far[i].wait_recv()
-                passed_on[i].start()
-            for copy in to_other + passed_on + mixes:
+            to_far[1].wait_recv()
+            passed_on[1].start()
+            for copy in to_other[:2] + passed_on[:2]:
                 copy.wait_recv()
             bd[...] = jnp.zeros_like(bd)
             for q in range(4):
@@ -205,24 +215,28 @@
             for tc in range(4):
                 for h in range(2):
                     low_rank(h, tc, xb[h, tc].reshape(128, 512))
+            to_far[2].wait_recv()
+            passed_on[2].start()
+
+        low = uacc[...].astype(BF)
+        scale = lax.rsqrt(jnp.sum(ssq[...], axis=1, keepdims=True) * (1.0 / 4096.0) + EPS)
+        for j in range(2):
+            g0 = j * 768
+            gates = acc[:, g0 : g0 + 384] + jnp.dot(low, bd[:, g0 : g0 + 384], preferred_element_type=F32)
+            uppers = acc[:, g0 + 384 : g0 + 768] + jnp.dot(low, bd[:, g0 + 384 : g0 + 768], preferred_element_type=F32)
+            weight = hs[j] * scale
+            for n in range(3):
+                half_gate = gates[:, n * 128 : n * 128 + 128] * (0.5 * scale)
+                hidden = (half_gate + half_gate * jnp.tanh(half_gate)) * (uppers[:, n * 128 : n * 128 + 128] * weight)
+                hbuf[:, j * 384 + n * 128 : j * 384 + n * 128 + 128] = hidden.astype(BF)
+        vbuf[...] = lax.dot_general(hbuf[...], adt[...], NT, preferred_element_type=F32).astype(BF)
+
+        @pl.when(s == 0)
+        def _():
+            for copy in (to_other[2], passed_on[2]):
+                copy.wait_recv()
             for copy in to_far + to_other + passed_on + mixes:
                 copy.wait_send()
-
-        low = uacc[...].astype(BF)
-        scale = lax.rsqrt(jnp.sum(ssq[...], axis=1, keepdims=True) * (1.0 / 4096.0) + EPS)
-        mixed = mixb[...].reshape(128, 128)
-        lanes = lax.broadcasted_iota(jnp.int32, (128, 128), 1)
-        for j in range(2):
-            here = jnp.sum(jnp.where(lanes == s * 16 + 2 * e + j, mixed, 0.0), axis=1, keepdims=True)
-            for n in range(3):
-                g0 = j * 768 + n * 128
-                u0 = g0 + 384
-                gate = acc[:, g0 : g0 + 128] + jnp.dot(low, bd[:, g0 : g0 + 128], preferred_element_type=F32)
-                upper = acc[:, u0 : u0 + 128] + jnp.dot(low, bd[:, u0 : u0 + 128], preferred_element_type=F32)
-                gate, upper = gate * scale, upper * scale
-                hidden = gate / (1.0 + jnp.exp(-gate)) * upper * here
-                hbuf[:, j * 384 + n * 128 : j * 384 + n * 128 + 128] = hidden.astype(BF)
-        vbuf[...] = lax.dot_general(hbuf[...], adt[...], NT, preferred_element_type=F32).astype(BF)
 
         for d in ORDER:
             tc = ts[d]
@@ -240,6 +254,12 @@
         for h in range(2):
             await_bytes(s2.at[0, pl.ds(0, 7)], a1s.at[h])
             await_bytes(po.at[0, pl.ds(0, 3)], a2s.at[h])
+
+        @pl.when(s > 0)
+        def _():
+            for h in range(2):
+                await_bytes(s2.at[0, pl.ds(0, 7)], b2s.at[h])
+
         for d in ORDER:
             for h in range(2):
                 await_bytes(rb.at[0, :, 0], b1r.at[h, d])
@@ -266,11 +286,11 @@
                 total = total + r2[h, 2 * d + dz].astype(F32)
             upd[:, cols] = total
             cur[:, cols] += total
-        for h in range(2):
-            await_bytes(s2.at[0, pl.ds(0, 7)], b2s.at[h])
         return carry
 
     lax.fori_loop(0, 3, step, 0)
+    for h in range(2):
+        await_bytes(s2.at[0, pl.ds(0, 7)], b2s.at[h])
     out_state[...] = cur[...]
     out_update[...] = upd[...]
 
@@ -288,7 +308,7 @@
         pltpu.VMEM((128, 1536), BF),
         pltpu.VMEM((64, 768), BF),
         pltpu.VMEM((4, 2, 16, 128), F32),
-        pltpu.VMEM((8, 128), F32),
+        pltpu.VMEM((2, 128, 128), F32),
         pltpu.VMEM((16, 1024), F32),
         pltpu.VMEM((16, 1024), F32),
         pltpu.VMEM((8, 1, 512), F32),

time: 92.4 us -> 90.8 us (0.983)
  Pallas kernels: 88.3 us -> 87 us
    pallas_call x1, Pallas kernels: 88.3 us -> 87 us  [per_device(): pl.pallas_call(kernel, out_shape=(shape, shape), in_specs=[hbm] * 13, out...]
where the time goes in v3:
time: 90.8 us; the launch traced here: 90.6 us
  Pallas kernels  87 us (96%)
  local copies, waits for them, and re-layouts  2.95 us (3%)
    pallas_call x1, Pallas kernels, per_device(): pl.pallas_call(kernel, out_shape=(shape, shape), in_specs=[hbm] * 13, out...  87 us
    unnamed x2, local copies, waits for them, and re-layouts  2.95 us

profile of v3, /device:TPU:0, one launch (start us, length us, event | category | flops | bytes accessed | tf_op | source)
XLA Modules:
  0.0 90.6 jit_solution(11690475590499129729)
XLA Ops:
  0.6 87.0 %shard_map.140 = (f32[16,1024]{1,0:T(8,128)}, f32[16,1024]{1,0:T(8,128)}) custom-call(bf16[16,1024]{1,0:T(8,128)(2,1)} %states_in.1, f32[32,128]{1,0:T(8,128)} %bitcast.3, s32[3,4,16]{2,1,0:T(4,128)} %bitcast.4, f32[3,4,16]{2,1,0:T(4,128)} %bitcast.5, bf16[2,8,4096]{2,1,0:T(8,128)(2,1)} %ga_in.1, bf16[2,8,384]{2,1,0:T(8,128)(2,1)} %gb_in.1, ...), custom_call_target="tpu_custom_call" | custom-call | tf_op jit(solution)/shard_map/pallas_call | solution.py:342
  87.7 1.5 %copy.17 = f32[16,1024]{1,0:T(8,128)} copy(f32[16,1024]{1,0:T(8,128)} %get-tuple-element.4) | data formatting | bytes 131072
  89.1 1.5 %copy.18 = f32[16,1024]{1,0:T(8,128)} copy(f32[16,1024]{1,0:T(8,128)} %get-tuple-element.5) | data formatting | bytes 131072

commit v4 on v3

--- a/solution.py
+++ b/solution.py
@@ -15,7 +15,7 @@
 
 def kernel(
     states_in, gain_in, ids_in, weights_in, ga_in, gb_in, ua_in, ub_in, da_in, db_in, gw, uw, dw,
-    out_state, out_update,
+    out,
     states, gain, ids, weights, ga, gb, ua, ub, da, db,
     w, wd, abuf, sbuf, bd, adt, mixb, hs, cur, upd, gs, gi, xb, acc, uacc, ssq, hbuf, vbuf, po, rb, s2, r2,
     isem, wsem, ad_s, ad_r, mx_s, mx_r, a1s, a1r, a2s, a2r, b1s, b1r, b2s, b2r,
@@ -67,7 +67,7 @@
     for j in range(2):
         loads.append((dw.at[j], wd.at[pl.ds(j * 384, 384)]))
     loads = [pltpu.make_async_copy(a, b, wsem.at[i]) for i, (a, b) in enumerate(loads)]
-    for copy in loads:
+    for copy in loads[:4]:
         copy.start()
 
     for copy in small:
@@ -146,6 +146,8 @@
         def _():
             for copy in mixes:
                 copy.wait_recv()
+            for copy in loads[4:]:
+                copy.start()
 
         mixed = mixb[...].reshape(128, 128)
         lanes = lax.broadcasted_iota(jnp.int32, (128, 128), 1)
@@ -291,8 +293,8 @@
     lax.fori_loop(0, 3, step, 0)
     for h in range(2):
         await_bytes(s2.at[0, pl.ds(0, 7)], b2s.at[h])
-    out_state[...] = cur[...]
-    out_update[...] = upd[...]
+    out[0] = cur[...]
+    out[1] = upd[...]
 
 
 def per_device(states, gain, ids, weights, gw, uw, dw, ga, gb, ua, ub, da, db):
@@ -338,15 +340,15 @@
         dma((2,)),
         dma((2,)),
     ]
-    shape = jax.ShapeDtypeStruct((16, 1024), F32)
-    return pl.pallas_call(
+    both = pl.pallas_call(
         kernel,
-        out_shape=(shape, shape),
+        out_shape=jax.ShapeDtypeStruct((2, 16, 1024), F32),
         in_specs=[hbm] * 13,
-        out_specs=(vmem, vmem),
+        out_specs=vmem,
         scratch_shapes=scratch,
         compiler_params=pltpu.CompilerParams(collective_id=0, has_side_effects=True, vmem_limit_bytes=62 << 20),
     )(*args)
+    return both[0], both[1]
 
 
 def solution(mesh):

time: 90.8 us -> 88.8 us (0.978)
  local copies, waits for them, and re-layouts: 2.95 us -> 1.53 us
    unnamed x2 -> x0, local copies, waits for them, and re-layouts: 2.95 us -> none
    squeeze x0 -> x1, local copies, waits for them, and re-layouts: none -> 1.53 us  [per_device(): return (both[0], both[1])]
where the time goes in v4:
time: 88.8 us; the launch traced here: 88.7 us
  Pallas kernels  86.5 us (97%)
  local copies, waits for them, and re-layouts  1.53 us (2%)
    pallas_call x1, Pallas kernels, per_device(): pl.pallas_call(kernel, out_shape=jax.ShapeDtypeStruct((2, 16, 1024), F32)...  86.5 us

profile of v4, /device:TPU:0, one launch (start us, length us, event | category | flops | bytes accessed | tf_op | source)
XLA Modules:
  0.0 88.7 jit_solution(6272150849435368907)
XLA Ops:
  0.6 86.5 %shard_map.140 = f32[2,16,1024]{2,1,0:T(8,128)} custom-call(bf16[16,1024]{1,0:T(8,128)(2,1)} %states_in.1, f32[32,128]{1,0:T(8,128)} %bitcast.7, s32[3,4,16]{2,1,0:T(4,128)} %bitcast.8, f32[3,4,16]{2,1,0:T(4,128)} %bitcast.9, bf16[2,8,4096]{2,1,0:T(8,128)(2,1)} %ga_in.1, bf16[2,8,384]{2,1,0:T(8,128)(2,1)} %gb_in.1, bf16[2,8,4096]{2,1,0:T(8,128)(2,1)} %ua_in.1, ...), custom_call_target="tpu_custom_call" | custom-call | tf_op jit(solution)/shard_map/pallas_call | solution.py:343
  87.1 1.5 %slice_bitcast_fusion = (f32[16,1024]{1,0:T(8,128)}, f32[16,1024]{1,0:T(8,128)}) fusion(f32[2,16,1024]{2,1,0:T(8,128)} %shard_map.140), kind=kLoop, calls=%fused_computation | loop fusion | bytes 262144 | tf_op jit(solution)/shard_map/squeeze | solution.py:351
